TPU v7x, 256 devices: a whole 4x4x8 slice. The times are simulated.
256 devices in a mesh: sub: 32 (over y, x, core), grp: 8 (over z).
Axes of the slice: x: 4, y: 4, z: 8, core: 2. Of those that a mesh axis runs over, the one named last changes fastest.
Arguments:
- residual: bfloat16 [8, 32, 1024, 512], P('grp', 'sub'), may hold values from -6 to 6
- face_order: int32 [8, 32, 1024], P('grp', 'sub'), may hold values from 0 to 1023, each once within a row
- stiffness: float32 [8, 32], replicated, may hold values from 1 to 100
- schur: bfloat16 [8, 32, 1024, 1024], P('grp', 'sub')
- local_inverse: bfloat16 [8, 32, 1024, 1024], P('grp', 'sub')
- coarse_basis: bfloat16 [8, 32, 1024, 128], P('grp', 'sub'), may hold values from -0.1875 to 0.1875
- coarse_map: int32 [8, 32, 128], P('grp', 'sub'), may hold values from 0 to 511, as said below
- level2_inverse: float32 [8, 512, 512], P('grp')
- level2_basis: float32 [8, 512, 128], P('grp'), may hold values from -0.25 to 0.25
- level2_map: int32 [8, 128], P('grp'), may hold values from 0 to 511, as said below
- level3_inverse: float32 [512, 512], replicated
Outputs:
- solution: bfloat16 [8, 32, 1024, 512], P('grp', 'sub')
- image: bfloat16 [8, 32, 1024, 512], P('grp', 'sub')
Inputs may be any that keep to these rules, and one draw needn't show every extreme that they name: `face_order`: each subdomain's row holds every number of 0 to 1023 once. `coarse_map`: within one subdomain the 128 entries are distinct, and each of a group's 512 level-2 coarse values is named by some subdomain of the group. `level2_map`: within one group the 128 entries are distinct, and each level-3 coarse value is named by some group.
All inputs are finite; a program needn't handle non-finite values.
Results may differ from a plain program's by a relative error of at most 0.0062.
Values may be sent and summed in bfloat16 or wider, within the bound.
A program may use at most 64 MiB of HBM per device.

v0:
```python
import jax
import jax.numpy as jnp
from jax import lax
from jax.sharding import PartitionSpec as P

highest = lax.Precision.HIGHEST


def extended(cells, sides, width):
    for axis, dim in sides:
        count = lax.axis_size(axis)
        ends = count - 1
        head = lax.slice_in_dim(cells, 0, width, axis=dim)
        tail = lax.slice_in_dim(cells, cells.shape[dim] - width, cells.shape[dim], axis=dim)
        cells = jnp.concatenate(
            [
                lax.ppermute(tail, axis, [(i, (i + 1) % count) for i in range(ends)]),
                cells,
                lax.ppermute(head, axis, [((i + 1) % count, i) for i in range(ends)]),
            ],
            axis=dim,
        )
    return cells


def face_weights(stiffness, group_index, member_index):
    group_count, member_count = stiffness.shape
    itself = stiffness[group_index, member_index]

    def share_of(other_group, other_member, present):
        neighbour = stiffness[
            jnp.clip(other_group, 0, group_count - 1), jnp.clip(other_member, 0, member_count - 1)
        ]
        return jnp.where(present, itself / (itself + neighbour), jnp.float32(1.0))

    return jnp.stack(
        [
            share_of(group_index, member_index - 1, member_index > 0),
            share_of(group_index, member_index + 1, member_index < member_count - 1),
            share_of(group_index - 1, member_index, group_index > 0),
            share_of(group_index + 1, member_index, group_index < group_count - 1),
        ]
    )


def shards(
    residual,
    face_order,
    stiffness,
    schur,
    local_inverse,
    coarse_basis,
    coarse_map,
    level2_inverse,
    level2_basis,
    level2_map,
    level3_inverse,
):
    resid_block = residual[0, 0]
    interface_size, columns = resid_block.shape
    face_size = interface_size // 4
    ordering = face_order[0, 0]
    inverse = jnp.argsort(ordering)
    group_index = lax.axis_index("grp")
    member_index = lax.axis_index("sub")
    weights = face_weights(stiffness, group_index, member_index)
    face_of = inverse // face_size
    dof_weight = jnp.sum(
        jnp.where(face_of[:, None] == jnp.arange(4)[None, :], weights[None, :], jnp.float32(0.0)),
        axis=1,
    )
    weighted = (dof_weight[:, None] * resid_block.astype(jnp.float32)).astype(jnp.bfloat16)
    contract_rows = (((0,), (0,)), ((), ()))
    coarse_base = coarse_basis[0, 0]
    coarse_res = lax.dot_general(
        coarse_base, weighted, contract_rows, preferred_element_type=jnp.float32
    )
    level2_size = level2_inverse.shape[1]
    local_map = coarse_map[0, 0]
    selector = (local_map[None, :] == jnp.arange(level2_size)[:, None]).astype(jnp.float32)
    contribution = jnp.dot(selector, coarse_res, precision=highest)
    group_base = level2_basis[0]
    group_map = level2_map[0]
    level3_size = level3_inverse.shape[0]
    selector_three = (group_map[None, :] == jnp.arange(level3_size)[:, None]).astype(jnp.float32)
    local_part = jnp.dot(local_inverse[0, 0], weighted, preferred_element_type=jnp.float32)
    group_inverse = level2_inverse[0]
    level2_res = lax.psum(contribution, "sub")
    group_terms = lax.dot_general(group_base, level2_res, contract_rows, precision=highest)
    level3_res = lax.psum(jnp.dot(selector_three, group_terms, precision=highest), "grp")
    level2_local = jnp.dot(group_inverse, level2_res, precision=highest)
    level3_sol = jnp.dot(level3_inverse, level3_res, precision=highest)
    level2_sol = level2_local + jnp.dot(group_base, level3_sol[group_map], precision=highest)
    coarse_part = jnp.dot(coarse_base.astype(jnp.float32), level2_sol[local_map], precision=highest)
    sendable = (dof_weight[:, None] * (local_part + coarse_part)).astype(jnp.bfloat16)
    face_blocks = sendable[ordering].reshape(4, face_size, columns)
    sub_padded = extended(face_blocks[0:2], (("sub", 0),), 1)
    grp_padded = extended(face_blocks[2:4], (("grp", 0),), 1)
    received = jnp.stack([sub_padded[0], sub_padded[3], grp_padded[0], grp_padded[3]])
    summed = (face_blocks.astype(jnp.float32) + received.astype(jnp.float32)).astype(jnp.bfloat16)
    solution = summed.reshape(interface_size, columns)[inverse]
    image = jnp.dot(schur[0, 0], solution, preferred_element_type=jnp.float32).astype(jnp.bfloat16)
    return (solution[None, None], image[None, None])


def solution(mesh):
    placed = (
        P("grp", "sub", None, None),
        P("grp", "sub", None),
        P(),
        P("grp", "sub", None, None),
        P("grp", "sub", None, None),
        P("grp", "sub", None, None),
        P("grp", "sub", None),
        P("grp", None, None),
        P("grp", None, None),
        P("grp", None),
        P(),
    )
    return jax.shard_map(
        shards,
        mesh=mesh,
        in_specs=placed,
        out_specs=(P("grp", "sub", None, None), P("grp", "sub", None, None)),
        check_vma=False,
    )
```

profile of v0, /device:TPU:8, one launch (start us, length us, event | category | flops | bytes accessed | tf_op | source)
XLA Modules:
  0.0 290.3 jit_solution(15084661443975097650)
XLA Ops:
  7.2 0.0 copy-start
  7.2 0.0 all-reduce.3.cloned.1.call-start
  7.2 1.6 fusion.33
  16.3 5.1 %sort.17 = (s32[1024]{0:T(1024)}, s32[1024]{0:T(1024)S(1)}) sort(s32[1024]{0:T(1024)} %bitcast.82, s32[1024]{0:T(1024)S(1)} %iota.13), dimensions={0}, to_apply=%region_0.0 | sort | flops 10240 | bytes 16384 | tf_op jit(solution)/shard_map/jit(argsort)/sort | solution.py:63
  21.4 0.0 copy-start.6
  21.4 0.1 pad_maximum_fusion.1
  21.5 0.0 copy-start.4
  21.5 0.1 select_reduce_fusion
  21.6 1.9 fusion.15
  23.6 2.2 fusion.24
  25.8 0.0 all-reduce.3.cloned.1.call-update
  25.8 0.0 copy-start.7
  25.8 0.0 copy-start.5
  25.8 0.0 all-reduce.5.cloned.1.call-start
  25.9 0.0 copy-done.6
  25.9 117.2 %all-reduce.3.cloned.1.call-done = f32[512,512]{1,0:T(8,128)} async-done(((f32[512,512]{1,0:T(8,128)}), f32[512,512]{1,0:T(8,128)}) %all-reduce.3.cloned.1.call-update) | async-done | bytes 1048592 | tf_op jit(solution)/shard_map/psum | solution.py:88
  143.2 0.0 copy-done.4
  143.2 3.0 %fusion.20 = f32[512,128]{1,0:T(8,128)S(1)} fusion(f32[512,512]{1,0:T(8,128)} %all-reduce.3.cloned.1.call-done, f32[1,512,128]{2,1,0:T(8,128)S(1)} %copy-done.4), kind=kOutput, calls=%fused_computation.28 | convolution fusion | flops 402653184 | bytes 1572864 | tf_op jit(solution)/shard_map/dot_general | solution.py:89
  146.2 1.6 fusion.25
  147.8 0.0 all-reduce.5.cloned.1.call-update
  147.8 0.0 copy-done.7
  147.8 0.0 copy-done.5
  147.9 0.0 copy-done
  147.9 0.0 copy-start.3
  147.9 4.2 %fusion.3 = f32[512,1024]{1,0:T(8,128)} fusion(bf16[1,1,1024,1024]{3,2,1,0:T(8,128)(2,1)S(1)} %copy-done, bf16[1,1,1024,512]{3,2,1,0:T(8,128)(2,1)} %param.11, f32[1024]{0:T(1024)S(1)} %select_reduce_fusion), kind=kOutput, calls=%fused_computation.8 | convolution fusion | flops 1075314688 | bytes 5246976 | tf_op jit(solution)/shard_map/dot_general | solution.py:86
  152.1 72.2 %all-reduce.5.cloned.1.call-done = f32[512,512]{1,0:T(8,128)} async-done(((f32[512,512]{1,0:T(8,128)}), f32[512,512]{1,0:T(8,128)}) %all-reduce.5.cloned.1.call-update) | async-done | bytes 1048592 | tf_op jit(solution)/shard_map/psum | solution.py:90
  224.3 0.0 copy-done.3
  224.3 5.7 %convolution_bitcast_fusion = f32[512,512]{0,1:T(8,128)} fusion(f32[512,512]{1,0:T(8,128)} %all-reduce.5.cloned.1.call-done, f32[512,512]{1,0:T(8,128)S(1)} %copy-done.3), kind=kOutput, calls=%fused_computation.15 | convolution fusion | flops 1610612736 | bytes 3145728 | tf_op jit(solution)/shard_map/dot_general | solution.py:92
  230.0 1.6 copy.17
  231.5 0.8 gather_fusion
  232.3 0.0 copy-start.2
  232.3 2.1 fusion.18
  234.4 0.0 copy-done.2
  234.4 5.7 %fusion.12 = f32[512,512]{0,1:T(8,128)} fusion(f32[512,512]{1,0:T(8,128)S(1)} %fusion.18, f32[512,512]{1,0:T(8,128)S(1)} %copy-done.2, f32[1,512,512]{2,1,0:T(8,128)} %param.18), kind=kOutput, calls=%fused_computation.17 | convolution fusion | flops 1610874880 | bytes 4194304 | tf_op jit(solution)/shard_map/dot_general | solution.py:91
  240.1 1.7 copy.18
  241.8 0.8 gather_fusion.1
  242.5 3.7 %fusion.11 = bf16[1024,512]{0,1:T(8,128)(2,1)} fusion(f32[512,1024]{1,0:T(8,128)} %fusion.3, f32[128,512]{1,0:T(8,128)S(1)} %gather_fusion.1, f32[1024]{0:T(1024)S(1)} %select_reduce_fusion, bf16[1,1,1024,128]{3,2,1,0:T(8,128)(2,1)} %param.16), kind=kOutput, calls=%fused_computation.14 | convolution fusion | flops 806879232 | bytes 3674112 | tf_op jit(solution)/shard_map/dot_general | solution.py:94
  246.3 1.5 copy.19
  247.8 5.1 %gather_fusion.2 = bf16[1024,512]{1,0:T(8,128)(2,1)} fusion(bf16[1024,512]{1,0:T(8,128)(2,1)S(1)} %copy.19, s32[1024]{0:T(1024)S(1)} %broadcast_clamp_fusion), kind=kCustom, calls=%fused_computation.2 | custom fusion | bytes 2101248 | tf_op jit(solution)/shard_map/gather | solution.py:96
  252.9 0.0 copy-start.1
  252.9 1.3 slice_bitcast_fusion.3
  254.2 1.9 collective-permute-start
  256.2 5.8 %collective-permute-start.1 = (bf16[1,256,512]{2,1,0:T(8,128)(2,1)S(1)}, bf16[1,256,512]{2,1,0:T(8,128)(2,1)S(1)}, u32[]{:S(2)}, u32[]{:S(2)}) collective-permute-start(bf16[1,256,512]{2,1,0:T(8,128)(2,1)S(1)} %get-tuple-element.12), channel_id=1, source_target_pairs={{8,0},{16,8},{24,16},{32,24},{40,32},{48,40},{56,48},{64,56},{72,6... | collective-permute-start | bytes 786440 | tf_op jit(solution)/shard_map/ppermute | solution.py:19
  261.9 3.1 %collective-permute-start.2 = (bf16[1,256,512]{2,1,0:T(8,128)(2,1)S(1)}, bf16[1,256,512]{2,1,0:T(8,128)(2,1)S(1)}, u32[]{:S(2)}, u32[]{:S(2)}) collective-permute-start(bf16[1,256,512]{2,1,0:T(8,128)(2,1)S(1)} %get-tuple-element.11), channel_id=1, source_target_pairs={{0,1},{1,2},{2,3},{3,4},{4,5},{5,6},{6,7},{8,9},{9,10},{10,11},{11... | collective-permute-start | bytes 786440 | tf_op jit(solution)/shard_map/ppermute | solution.py:17
  265.1 1.3 collective-permute-start.3
  266.4 0.0 collective-permute-done
  266.4 0.0 collective-permute-done.1
  266.4 2.5 collective-permute-done.2
  268.9 4.4 %collective-permute-done.3 = bf16[1,256,512]{2,1,0:T(8,128)(2,1)S(1)} collective-permute-done((bf16[1,256,512]{2,1,0:T(8,128)(2,1)S(1)}, bf16[1,256,512]{2,1,0:T(8,128)(2,1)S(1)}, u32[]{:S(2)}, u32[]{:S(2)}) %collective-permute-start.3) | collective-permute-done | bytes 262176 | tf_op jit(solution)/shard_map/ppermute | solution.py:19
  273.3 0.1 pad_maximum_fusion
  273.5 0.0 copy-done.1
  273.5 0.4 fusion
  273.9 5.1 %gather_fusion.3 = bf16[1024,512]{1,0:T(8,128)(2,1)} fusion(bf16[1024,512]{1,0:T(8,128)(2,1)S(1)} %fusion, s32[1024]{0:T(1024)S(1)} %get-tuple-element.14), kind=kCustom, calls=%fused_computation.3 | custom fusion | bytes 2101248 | tf_op jit(solution)/shard_map/gather | solution.py:101
  278.9 3.2 %fusion.8 = bf16[1,1,1024,512]{2,3,1,0:T(8,128)(2,1)S(1)} fusion(bf16[1024,512]{1,0:T(8,128)(2,1)} %gather_fusion.3, bf16[1,1,1024,1024]{3,2,1,0:T(8,128)(2,1)} %param.14), kind=kOutput, calls=%fused_computation.13 | convolution fusion | flops 1074266112 | bytes 4194304 | tf_op jit(solution)/shard_map/dot_general | solution.py:102
  282.2 1.3 copy.20
  (8 shorter events, 0.0 us)
Async XLA Ops:
  7.2 140.7 %copy-start = (bf16[1,1,1024,1024]{3,2,1,0:T(8,128)(2,1)S(1)}, bf16[1,1,1024,1024]{3,2,1,0:T(8,128)(2,1)}, u32[]{:S(2)}) copy-start(bf16[1,1,1024,1024]{3,2,1,0:T(8,128)(2,1)} %param.15) | copy-start | bytes 6291460
  7.2 136.0 %all-reduce.3.cloned.1.call-start = ((), (), s32[]{:S(2)}) async-start(), calls=%async_computation | async-start | bytes 2097152 | tf_op jit(solution)/shard_map/psum | solution.py:88
  21.4 4.5 %copy-start.6 = (s32[1,128]{1,0:T(1,128)S(1)}, s32[1,128]{1,0:T(1,128)}, u32[]{:S(2)}) copy-start(s32[1,128]{1,0:T(1,128)} %param.20) | copy-start | bytes 1540
  21.5 121.6 %copy-start.4 = (f32[1,512,128]{2,1,0:T(8,128)S(1)}, f32[1,512,128]{2,1,0:T(8,128)}, u32[]{:S(2)}) copy-start(f32[1,512,128]{2,1,0:T(8,128)} %param.19) | copy-start | bytes 786436
  25.8 122.0 %copy-start.7 = (s32[1,1,128]{2,1,0:T(1,128)S(1)}, s32[1,1,128]{2,1,0:T(1,128)}, u32[]{:S(2)}) copy-start(s32[1,1,128]{2,1,0:T(1,128)} %param.17) | copy-start | bytes 1540
  25.8 122.0 %copy-start.5 = (s32[1,1,1024]{2,1,0:T(1,128)S(1)}, s32[1,1,1024]{2,1,0:T(1,128)}, u32[]{:S(2)}) copy-start(s32[1,1,1024]{2,1,0:T(1,128)} %param.12) | copy-start | bytes 12292
  25.8 198.5 %all-reduce.5.cloned.1.call-start = ((), (), s32[]{:S(2)}) async-start(), calls=%async_computation.1 | async-start | bytes 2097152 | tf_op jit(solution)/shard_map/psum | solution.py:90
  147.9 76.4 %copy-start.3 = (f32[512,512]{1,0:T(8,128)S(1)}, f32[512,512]{1,0:T(8,128)}, u32[]{:S(2)}) copy-start(f32[512,512]{1,0:T(8,128)} %param.21) | copy-start | bytes 3145732
  232.3 2.1 copy-start.2
  252.9 20.6 %copy-start.1 = (bf16[1024,512]{1,0:T(8,128)(2,1)S(1)}, bf16[1024,512]{1,0:T(8,128)(2,1)}, u32[]{:S(2)}) copy-start(bf16[1024,512]{1,0:T(8,128)(2,1)} %gather_fusion.2) | copy-start | bytes 3145732
  254.2 12.1 %collective-permute-start = (bf16[1,256,512]{2,1,0:T(8,128)(2,1)S(1)}, bf16[1,256,512]{2,1,0:T(8,128)(2,1)S(1)}, u32[]{:S(2)}, u32[]{:S(2)}) collective-permute-start(bf16[1,256,512]{2,1,0:T(8,128)(2,1)S(1)} %get-tuple-element.10), channel_id=1, source_target_pairs={{0,8},{8,16},{16,24},{24,32},{32,40},{40,48},{48,56},{56,64},{64,7... | collective-permute-start | bytes 786440 | tf_op jit(solution)/shard_map/ppermute | solution.py:17
  256.2 10.2 %collective-permute-start.1 = (bf16[1,256,512]{2,1,0:T(8,128)(2,1)S(1)}, bf16[1,256,512]{2,1,0:T(8,128)(2,1)S(1)}, u32[]{:S(2)}, u32[]{:S(2)}) collective-permute-start(bf16[1,256,512]{2,1,0:T(8,128)(2,1)S(1)} %get-tuple-element.12), channel_id=1, source_target_pairs={{8,0},{16,8},{24,16},{32,24},{40,32},{48,40},{56,48},{64,56},{72,6... | collective-permute-start | bytes 786440 | tf_op jit(solution)/shard_map/ppermute | solution.py:19
  261.9 7.0 %collective-permute-start.2 = (bf16[1,256,512]{2,1,0:T(8,128)(2,1)S(1)}, bf16[1,256,512]{2,1,0:T(8,128)(2,1)S(1)}, u32[]{:S(2)}, u32[]{:S(2)}) collective-permute-start(bf16[1,256,512]{2,1,0:T(8,128)(2,1)S(1)} %get-tuple-element.11), channel_id=1, source_target_pairs={{0,1},{1,2},{2,3},{3,4},{4,5},{5,6},{6,7},{8,9},{9,10},{10,11},{11... | collective-permute-start | bytes 786440 | tf_op jit(solution)/shard_map/ppermute | solution.py:17
  265.1 8.3 %collective-permute-start.3 = (bf16[1,256,512]{2,1,0:T(8,128)(2,1)S(1)}, bf16[1,256,512]{2,1,0:T(8,128)(2,1)S(1)}, u32[]{:S(2)}, u32[]{:S(2)}) collective-permute-start(bf16[1,256,512]{2,1,0:T(8,128)(2,1)S(1)} %get-tuple-element.13), channel_id=1, source_target_pairs={{1,0},{2,1},{3,2},{4,3},{5,4},{6,5},{7,6},{9,8},{10,9},{11,10},{12... | collective-permute-start | bytes 786440 | tf_op jit(solution)/shard_map/ppermute | solution.py:19
Sparse Core Ops, SparseCore 0:
  25.9 117.1 all-reduce.2
  147.9 76.3 all-reduce.4
where the time goes:
time: 291 us; the launch traced here: 290 us
  waiting for transfers between devices  196 us (67%)
  matrix products  33.3 us (11%)
  between operations  21.9 us (8%)
  local copies, waits for them, and re-layouts  20.7 us (7%)
  starting transfers between devices  12.2 us (4%)
  other arithmetic  5.76 us (2%)
    psum x1, waiting for transfers between devices, shards(): level2_res = lax.psum(contribution, 'sub')  117 us
    psum x1, waiting for transfers between devices, shards(): lax.psum(jnp.dot(selector_three, group_terms, precision=highest), 'grp')  72.2 us
    ppermute x2, starting transfers between devices, extended(): lax.ppermute(head, axis, [((i + 1) % count, i) for i in range(ends)])  7.04 us
  transfers between devices with their start and end apart: 6, of which 4 were waited for; matrix products, arithmetic and copies ran while one was open for 1% of the time, Pallas kernels for 0%

commit v1 on v0

--- a/solution.py
+++ b/solution.py
@@ -87,7 +87,9 @@
     group_inverse = level2_inverse[0]
     level2_res = lax.psum(contribution, "sub")
     group_terms = lax.dot_general(group_base, level2_res, contract_rows, precision=highest)
-    level3_res = lax.psum(jnp.dot(selector_three, group_terms, precision=highest), "grp")
+    block = jnp.dot(selector_three, group_terms, precision=highest)
+    blocks = lax.all_gather(block, "grp")
+    level3_res = jnp.sum(blocks, axis=0)
     level2_local = jnp.dot(group_inverse, level2_res, precision=highest)
     level3_sol = jnp.dot(level3_inverse, level3_res, precision=highest)
     level2_sol = level2_local + jnp.dot(group_base, level3_sol[group_map], precision=highest)

time: 291 us -> 313 us (1.076)
  waiting for transfers between devices: 196 us -> 215 us
  other arithmetic: 5.76 us -> 10.3 us
    all_gather x0 -> x1, waiting for transfers between devices: none -> 90.5 us  [shards(): blocks = lax.all_gather(block, 'grp')]
    psum x1 -> x0, waiting for transfers between devices: 72.2 us -> none  [shards(): lax.psum(jnp.dot(selector_three, group_terms, precision=highest), 'grp')]
    reduce_sum x0 -> x1, other arithmetic: none -> 4.49 us  [shards(): level3_res = jnp.sum(blocks, axis=0)]
  transfers between devices with their start and end apart: 6 -> 6, of which waited for: 4 -> 5; matrix products, arithmetic and copies ran while one was open for 1% -> 1% of each run, Pallas kernels for 0% -> 0%
where the time goes in v1:
time: 313 us; the launch traced here: 311 us
  waiting for transfers between devices  215 us (69%)
  matrix products  33.4 us (11%)
  between operations  21.7 us (7%)
  local copies, waits for them, and re-layouts  20.5 us (7%)
  starting transfers between devices  10.7 us (3%)
  other arithmetic  10.3 us (3%)
    psum x1, waiting for transfers between devices, shards(): level2_res = lax.psum(contribution, 'sub')  117 us
    all_gather x1, waiting for transfers between devices, shards(): blocks = lax.all_gather(block, 'grp')  90.5 us
    ppermute x2, starting transfers between devices, extended(): lax.ppermute(head, axis, [((i + 1) % count, i) for i in range(ends)])  7.04 us
  transfers between devices with their start and end apart: 6, of which 5 were waited for; matrix products, arithmetic and copies ran while one was open for 1% of the time, Pallas kernels for 0%

profile of v1, /device:TPU:8, one launch (start us, length us, event | category | flops | bytes accessed | tf_op | source)
XLA Modules:
  0.0 311.4 jit_solution(3058454516985966188)
XLA Ops:
  7.2 0.0 copy-start
  7.2 0.0 all-reduce.2.cloned.1.call-start
  7.2 1.5 fusion.33
  16.1 5.1 %sort.17 = (s32[1024]{0:T(1024)}, s32[1024]{0:T(1024)S(1)}) sort(s32[1024]{0:T(1024)} %bitcast.84, s32[1024]{0:T(1024)S(1)} %iota.13), dimensions={0}, to_apply=%region_0.0 | sort | flops 10240 | bytes 16384 | tf_op jit(solution)/shard_map/jit(argsort)/sort | solution.py:63
  21.2 0.0 copy-start.3
  21.2 0.1 pad_maximum_fusion.1
  21.3 0.1 select_reduce_fusion
  21.4 1.9 fusion.15
  23.4 0.0 copy-start.5
  23.4 2.2 fusion.24
  25.6 0.0 all-reduce.2.cloned.1.call-update
  25.6 0.0 copy-start.6
  25.6 0.0 copy-start.4
  25.6 0.0 all-gather.3.cloned.1.call-start
  25.7 117.2 %all-reduce.2.cloned.1.call-done = f32[512,512]{1,0:T(8,128)} async-done(((f32[512,512]{1,0:T(8,128)}), f32[512,512]{1,0:T(8,128)}) %all-reduce.2.cloned.1.call-update) | async-done | bytes 1048592 | tf_op jit(solution)/shard_map/psum | solution.py:88
  142.9 0.0 copy-done.3
  142.9 3.0 fusion.20
  145.9 0.0 copy-done.5
  145.9 1.6 fusion.25
  147.5 0.0 all-gather.3.cloned.1.call-update
  147.6 0.0 copy-done.6
  147.6 0.0 copy-done.4
  147.6 0.0 copy-done
  147.7 4.1 %fusion.3 = f32[512,1024]{1,0:T(8,128)} fusion(bf16[1,1,1024,1024]{3,2,1,0:T(8,128)(2,1)S(1)} %copy-done, bf16[1,1,1024,512]{3,2,1,0:T(8,128)(2,1)} %param.11, f32[1024]{0:T(1024)S(1)} %select_reduce_fusion), kind=kOutput, calls=%fused_computation.8 | convolution fusion | flops 1075314688 | bytes 5246976 | tf_op jit(solution)/shard_map/dot_general | solution.py:86
  151.8 90.5 %all-gather.3.cloned.1.call-done = f32[4096,512]{1,0:T(8,128)} async-done(((f32[512,512]{1,0:T(8,128)}), f32[4096,512]{1,0:T(8,128)}) %all-gather.3.cloned.1.call-update) | async-done | bytes 8388624 | tf_op jit(solution)/shard_map/all_gather | solution.py:91
  242.3 4.5 %reduce_sum.19 = f32[512,512]{1,0:T(8,128)S(1)} reduce(f32[8,512,512]{2,1,0:T(8,128)} %bitcast.82, f32[]{:T(128)} %constant.49.clone.1), dimensions={0}, to_apply=%region_3.4 | reduce | flops 1835008 | bytes 9437188 | tf_op jit(solution)/shard_map/reduce_sum | solution.py:92
  246.8 5.7 %convolution_bitcast_fusion = f32[512,512]{0,1:T(8,128)} fusion(f32[512,512]{1,0:T(8,128)S(1)} %reduce_sum.19, f32[512,512]{1,0:T(8,128)} %param.21), kind=kOutput, calls=%fused_computation.15 | convolution fusion | flops 1610612736 | bytes 3145728 | tf_op jit(solution)/shard_map/dot_general | solution.py:94
  252.5 1.6 copy.17
  254.0 0.8 gather_fusion
  254.8 0.0 copy-start.2
  254.8 2.1 fusion.18
  256.9 0.0 copy-done.2
  256.9 5.9 %fusion.12 = f32[512,512]{0,1:T(8,128)} fusion(f32[512,512]{1,0:T(8,128)S(1)} %fusion.18, f32[512,512]{1,0:T(8,128)S(1)} %copy-done.2, f32[1,512,512]{2,1,0:T(8,128)} %param.18), kind=kOutput, calls=%fused_computation.17 | convolution fusion | flops 1610874880 | bytes 4194304 | tf_op jit(solution)/shard_map/dot_general | solution.py:93
  262.7 1.6 copy.18
  264.3 0.8 gather_fusion.1
  265.1 3.7 %fusion.11 = bf16[1024,512]{0,1:T(8,128)(2,1)} fusion(f32[512,1024]{1,0:T(8,128)} %fusion.3, f32[128,512]{1,0:T(8,128)S(1)} %gather_fusion.1, f32[1024]{0:T(1024)S(1)} %select_reduce_fusion, bf16[1,1,1024,128]{3,2,1,0:T(8,128)(2,1)} %param.16), kind=kOutput, calls=%fused_computation.14 | convolution fusion | flops 806879232 | bytes 3674112 | tf_op jit(solution)/shard_map/dot_general | solution.py:96
  268.8 1.5 copy.19
  270.3 5.1 %gather_fusion.2 = bf16[1024,512]{1,0:T(8,128)(2,1)} fusion(bf16[1024,512]{1,0:T(8,128)(2,1)S(1)} %copy.19, s32[1024]{0:T(1024)S(1)} %broadcast_clamp_fusion), kind=kCustom, calls=%fused_computation.2 | custom fusion | bytes 2101248 | tf_op jit(solution)/shard_map/gather | solution.py:98
  275.4 0.0 copy-start.1
  275.4 1.3 slice_bitcast_fusion.3
  276.7 1.9 collective-permute-start
  278.7 5.8 %collective-permute-start.1 = (bf16[1,256,512]{2,1,0:T(8,128)(2,1)S(1)}, bf16[1,256,512]{2,1,0:T(8,128)(2,1)S(1)}, u32[]{:S(2)}, u32[]{:S(2)}) collective-permute-start(bf16[1,256,512]{2,1,0:T(8,128)(2,1)S(1)} %get-tuple-element.12), channel_id=1, source_target_pairs={{8,0},{16,8},{24,16},{32,24},{40,32},{48,40},{56,48},{64,56},{72,6... | collective-permute-start | bytes 786440 | tf_op jit(solution)/shard_map/ppermute | solution.py:19
  284.4 1.7 collective-permute-start.2
  286.1 1.3 collective-permute-start.3
  287.4 0.0 collective-permute-done
  287.4 0.9 collective-permute-done.1
  288.3 1.7 collective-permute-done.2
  290.0 4.4 %collective-permute-done.3 = bf16[1,256,512]{2,1,0:T(8,128)(2,1)S(1)} collective-permute-done((bf16[1,256,512]{2,1,0:T(8,128)(2,1)S(1)}, bf16[1,256,512]{2,1,0:T(8,128)(2,1)S(1)}, u32[]{:S(2)}, u32[]{:S(2)}) %collective-permute-start.3) | collective-permute-done | bytes 262176 | tf_op jit(solution)/shard_map/ppermute | solution.py:19
  294.4 0.1 pad_maximum_fusion
  294.5 0.0 copy-done.1
  294.5 0.4 fusion
  294.9 5.1 %gather_fusion.3 = bf16[1024,512]{1,0:T(8,128)(2,1)} fusion(bf16[1024,512]{1,0:T(8,128)(2,1)S(1)} %fusion, s32[1024]{0:T(1024)S(1)} %get-tuple-element.14), kind=kCustom, calls=%fused_computation.3 | custom fusion | bytes 2101248 | tf_op jit(solution)/shard_map/gather | solution.py:103
  300.0 3.2 %fusion.8 = bf16[1,1,1024,512]{2,3,1,0:T(8,128)(2,1)S(1)} fusion(bf16[1024,512]{1,0:T(8,128)(2,1)} %gather_fusion.3, bf16[1,1,1024,1024]{3,2,1,0:T(8,128)(2,1)} %param.14), kind=kOutput, calls=%fused_computation.13 | convolution fusion | flops 1074266112 | bytes 4194304 | tf_op jit(solution)/shard_map/dot_general | solution.py:104
  303.2 1.3 copy.20
  (8 shorter events, 0.0 us)
Async XLA Ops:
  7.2 140.5 %copy-start = (bf16[1,1,1024,1024]{3,2,1,0:T(8,128)(2,1)S(1)}, bf16[1,1,1024,1024]{3,2,1,0:T(8,128)(2,1)}, u32[]{:S(2)}) copy-start(bf16[1,1,1024,1024]{3,2,1,0:T(8,128)(2,1)} %param.15) | copy-start | bytes 6291460
  7.2 135.7 %all-reduce.2.cloned.1.call-start = ((), (), s32[]{:S(2)}) async-start(), calls=%async_computation | async-start | bytes 2097152 | tf_op jit(solution)/shard_map/psum | solution.py:88
  21.2 121.7 %copy-start.3 = (f32[1,512,128]{2,1,0:T(8,128)S(1)}, f32[1,512,128]{2,1,0:T(8,128)}, u32[]{:S(2)}) copy-start(f32[1,512,128]{2,1,0:T(8,128)} %param.19) | copy-start | bytes 786436
  23.4 122.6 %copy-start.5 = (s32[1,128]{1,0:T(1,128)S(1)}, s32[1,128]{1,0:T(1,128)}, u32[]{:S(2)}) copy-start(s32[1,128]{1,0:T(1,128)} %param.20) | copy-start | bytes 1540
  25.6 122.0 %copy-start.6 = (s32[1,1,128]{2,1,0:T(1,128)S(1)}, s32[1,1,128]{2,1,0:T(1,128)}, u32[]{:S(2)}) copy-start(s32[1,1,128]{2,1,0:T(1,128)} %param.17) | copy-start | bytes 1540
  25.6 122.0 %copy-start.4 = (s32[1,1,1024]{2,1,0:T(1,128)S(1)}, s32[1,1,1024]{2,1,0:T(1,128)}, u32[]{:S(2)}) copy-start(s32[1,1,1024]{2,1,0:T(1,128)} %param.12) | copy-start | bytes 12292
  25.6 216.7 %all-gather.3.cloned.1.call-start = ((), (), s32[]{:S(2)}) async-start(), calls=%async_computation.1 | async-start | bytes 9437184 | tf_op jit(solution)/shard_map/all_gather | solution.py:91
  254.8 2.1 copy-start.2
  275.4 19.1 %copy-start.1 = (bf16[1024,512]{1,0:T(8,128)(2,1)S(1)}, bf16[1024,512]{1,0:T(8,128)(2,1)}, u32[]{:S(2)}) copy-start(bf16[1024,512]{1,0:T(8,128)(2,1)} %gather_fusion.2) | copy-start | bytes 3145732
  276.7 10.7 %collective-permute-start = (bf16[1,256,512]{2,1,0:T(8,128)(2,1)S(1)}, bf16[1,256,512]{2,1,0:T(8,128)(2,1)S(1)}, u32[]{:S(2)}, u32[]{:S(2)}) collective-permute-start(bf16[1,256,512]{2,1,0:T(8,128)(2,1)S(1)} %get-tuple-element.10), channel_id=1, source_target_pairs={{0,8},{8,16},{16,24},{24,32},{32,40},{40,48},{48,56},{56,64},{64,7... | collective-permute-start | bytes 786440 | tf_op jit(solution)/shard_map/ppermute | solution.py:17
  278.7 9.6 %collective-permute-start.1 = (bf16[1,256,512]{2,1,0:T(8,128)(2,1)S(1)}, bf16[1,256,512]{2,1,0:T(8,128)(2,1)S(1)}, u32[]{:S(2)}, u32[]{:S(2)}) collective-permute-start(bf16[1,256,512]{2,1,0:T(8,128)(2,1)S(1)} %get-tuple-element.12), channel_id=1, source_target_pairs={{8,0},{16,8},{24,16},{32,24},{40,32},{48,40},{56,48},{64,56},{72,6... | collective-permute-start | bytes 786440 | tf_op jit(solution)/shard_map/ppermute | solution.py:19
  284.4 5.5 %collective-permute-start.2 = (bf16[1,256,512]{2,1,0:T(8,128)(2,1)S(1)}, bf16[1,256,512]{2,1,0:T(8,128)(2,1)S(1)}, u32[]{:S(2)}, u32[]{:S(2)}) collective-permute-start(bf16[1,256,512]{2,1,0:T(8,128)(2,1)S(1)} %get-tuple-element.11), channel_id=1, source_target_pairs={{0,1},{1,2},{2,3},{3,4},{4,5},{5,6},{6,7},{8,9},{9,10},{10,11},{11... | collective-permute-start | bytes 786440 | tf_op jit(solution)/shard_map/ppermute | solution.py:17
  286.1 8.3 %collective-permute-start.3 = (bf16[1,256,512]{2,1,0:T(8,128)(2,1)S(1)}, bf16[1,256,512]{2,1,0:T(8,128)(2,1)S(1)}, u32[]{:S(2)}, u32[]{:S(2)}) collective-permute-start(bf16[1,256,512]{2,1,0:T(8,128)(2,1)S(1)} %get-tuple-element.13), channel_id=1, source_target_pairs={{1,0},{2,1},{3,2},{4,3},{5,4},{6,5},{7,6},{9,8},{10,9},{11,10},{12... | collective-permute-start | bytes 786440 | tf_op jit(solution)/shard_map/ppermute | solution.py:19
Sparse Core Ops, SparseCore 0:
  25.7 117.1 all-reduce.1
  147.7 94.5 all-gather.2
